TPU v7x, 32 devices: a whole 2x2x4 slice. The times are simulated.
32 devices in a mesh: blk: 8 (over y, x, core), off: 4 (over z).
Axes of the slice: x: 2, y: 2, z: 4, core: 2. Of those that a mesh axis runs over, the one named last changes fastest.
Arguments:
- coefficients: bfloat16 [128, 32, 128], P('blk', 'off'), may hold values from -12 to 12
Outputs:
- smoothed: float32 [128, 32, 128], P(('blk', 'off'))
- log_degree: float32 [128], P(('blk', 'off'))
All inputs are finite; a program needn't handle non-finite values.
Results may differ from a plain program's by a relative error of at most 0.005.
Values may be sent and summed in bfloat16 or wider, within the bound.
No kernel may reach another device: no remote copies, remote signals or barrier semaphores. Data moves between devices by JAX's collectives and lax.ppermute only.
A program may use at most 64 MiB of HBM per device.

v0:
```python
import math
import jax
import jax.numpy as jnp
from jax import lax
from jax.sharding import PartitionSpec as P

epsilon = 1e-06
concentration = 40.0


def shifted(array, axis, by):
    count = lax.axis_size(axis)
    return lax.ppermute(array, axis, [(i, (i + by) % count) for i in range(count)])


def angle_tables(angular):
    half_width = angular // 2
    frequency = jnp.arange(half_width, dtype=jnp.int32)
    shifts = jnp.arange(angular, dtype=jnp.int32)
    product = frequency[:, None] * shifts[None, :] % angular
    phase = product.astype(jnp.float32) * (2.0 * math.pi / angular)
    forward = jnp.concatenate([jnp.cos(phase), -jnp.sin(phase)], axis=0)
    return (forward, forward.T)


def inverse_norms(block_values):
    values = block_values.astype(jnp.float32)
    return lax.rsqrt(jnp.sum(values * values, axis=(1, 2)) + epsilon)


def tile_terms(own_block, own_inverse, other_block, offset, forward, backward):
    row_count = own_block.shape[0]
    half_width = own_block.shape[2] // 2
    highest = lax.Precision.HIGHEST
    other_inverse = inverse_norms(other_block)
    swapped = jnp.concatenate(
        [other_block[:, :, half_width:], other_block[:, :, :half_width]], axis=2
    )
    direct = jnp.einsum("irc,jrc->ijc", own_block, other_block, preferred_element_type=jnp.float32)
    mixed_terms = jnp.einsum("irc,jrc->ijc", own_block, swapped, preferred_element_type=jnp.float32)
    real_part = direct[:, :, :half_width] + direct[:, :, half_width:]
    imag_part = mixed_terms[:, :, half_width:] - mixed_terms[:, :, :half_width]
    cross_spectrum = jnp.concatenate([real_part, imag_part], axis=2).reshape(
        row_count * row_count, -1
    )
    correlation = jnp.dot(
        cross_spectrum, forward, precision=highest, preferred_element_type=jnp.float32
    )
    correlation = correlation.reshape(row_count, row_count, -1)
    cosine = correlation * own_inverse[:, None, None] * other_inverse[None, :, None]
    same_image = jnp.arange(row_count)[:, None] == jnp.arange(row_count)[None, :]
    keep_mask = jnp.where(jnp.logical_and(offset == 0, same_image), 0.0, 1.0).astype(jnp.float32)
    weights = jnp.exp(concentration * cosine) * keep_mask[:, :, None]
    spectral = jnp.dot(
        weights.reshape(row_count * row_count, -1),
        backward,
        precision=highest,
        preferred_element_type=jnp.float32,
    ).reshape(row_count, row_count, -1)
    degree = jnp.sum(spectral[:, :, 0], axis=1)
    rounded = spectral.astype(jnp.bfloat16)
    weight_real = jnp.concatenate([rounded[:, :, :half_width], rounded[:, :, :half_width]], axis=2)
    weight_imag = jnp.concatenate([-rounded[:, :, half_width:], rounded[:, :, half_width:]], axis=2)
    filtered = jnp.einsum(
        "ijc,jrc->irc", weight_real, other_block, preferred_element_type=jnp.float32
    )
    filtered = filtered + jnp.einsum(
        "ijc,jrc->irc", weight_imag, swapped, preferred_element_type=jnp.float32
    )
    return (filtered, degree)


def body(coefficients):
    own_block = lax.all_gather(coefficients, "off", axis=1, tiled=True)
    own_inverse = inverse_norms(own_block)
    row_count, radial, angular = own_block.shape
    forward, backward = angle_tables(angular)
    ranges = lax.axis_size("off")
    per_range = min(8, lax.axis_size("blk") // ranges)
    range_index = lax.axis_index("off")
    range_base = range_index * per_range
    packet = own_block
    packet = shifted(packet, "blk", -(per_range // 2))
    for bit_number in range(ranges.bit_length() - 1):
        moved_packet = shifted(packet, "blk", -(per_range << bit_number))
        chosen = range_index // (1 << bit_number) % 2 == 1
        packet = jnp.where(chosen, moved_packet, packet)
    empty_sum = jnp.zeros((row_count, radial, angular), jnp.float32)
    empty_degree = jnp.zeros((row_count,), jnp.float32)
    centre = range_base + per_range // 2
    lower_block = shifted(packet, "blk", 1)

    def advance_both(step, loop_state):
        filtered, degree, upper_block, lower_part = loop_state
        upper_terms = tile_terms(
            own_block, own_inverse, upper_block, centre + step, forward, backward
        )
        lower_terms = tile_terms(
            own_block, own_inverse, lower_part, centre - 1 - step, forward, backward
        )
        upper_block = shifted(upper_block, "blk", -1)
        lower_part = shifted(lower_part, "blk", 1)
        return (
            filtered + upper_terms[0] + lower_terms[0],
            degree + upper_terms[1] + lower_terms[1],
            upper_block,
            lower_part,
        )

    last_step = per_range // 2 - 1
    filtered, degree, upper_block, lower_block = lax.fori_loop(
        0, last_step, advance_both, (empty_sum, empty_degree, packet, lower_block)
    )
    upper_terms = tile_terms(
        own_block, own_inverse, upper_block, centre + last_step, forward, backward
    )
    lower_terms = tile_terms(
        own_block, own_inverse, lower_block, centre - 1 - last_step, forward, backward
    )
    filtered = filtered + upper_terms[0] + lower_terms[0]
    degree = degree + upper_terms[1] + lower_terms[1]
    totals = (
        lax.psum_scatter(filtered, "off", scatter_dimension=0, tiled=True),
        lax.psum_scatter(degree, "off", scatter_dimension=0, tiled=True),
    )
    smoothed = totals[0] / totals[1][:, None, None]
    return (smoothed, jnp.log(totals[1]))


def solution(mesh):
    return jax.shard_map(
        body,
        mesh=mesh,
        in_specs=(P("blk", "off", None),),
        out_specs=(P(("blk", "off"), None, None), P(("blk", "off"))),
        check_vma=False,
    )
```

profile of v0, /device:TPU:0, one launch (start us, length us, event | category | flops | bytes accessed | tf_op | source)
XLA Modules:
  0.0 91.2 jit_solution(6162711789580707457)
XLA Ops:
  7.2 1.0 %copy.17 = bf16[16,8,128]{0,1,2:T(8,128)(2,1)S(1)} copy(bf16[16,8,128]{2,1,0:T(8,128)(2,1)} %param.1) | data formatting | bytes 65536 | tf_op args[0]
  8.2 23.4 %all_gather.3 = bf16[16,32,128]{0,1,2:T(8,128)(2,1)S(1)} all-gather(bf16[16,8,128]{0,1,2:T(8,128)(2,1)S(1)} %copy.17), channel_id=1, replica_groups=mesh['blk'=8,'off'=4] {'off'}, dimensions={1}, use_global_device_ids=true | all-gather | bytes 163840 | tf_op jit(solution)/shard_map/all_gather | solution.py:74
  31.6 1.2 %copy.18 = bf16[16,32,128]{2,1,0:T(8,128)(2,1)S(1)} copy(bf16[16,32,128]{0,1,2:T(8,128)(2,1)S(1)} %all_gather.3) | data formatting | bytes 262144 | tf_op jit(solution)/shard_map/all_gather | solution.py:74
  32.8 1.2 %collective-permute-start = (bf16[16,32,128]{2,1,0:T(8,128)(2,1)S(1)}, bf16[16,32,128]{2,1,0:T(8,128)(2,1)S(1)}, u32[]{:S(2)}, u32[]{:S(2)}) collective-permute-start(bf16[16,32,128]{2,1,0:T(8,128)(2,1)S(1)} %copy.18), channel_id=1, source_target_pairs={{0,28},{4,0},{8,4},{12,8},{16,12},{20,16},{24,20},{28,24},{1,29},{... | collective-permute-start | bytes 393224 | tf_op jit(solution)/shard_map/ppermute | solution.py:13
  34.0 0.6 multiply_reduce_fusion
  34.5 2.0 %collective-permute-done = bf16[16,32,128]{2,1,0:T(8,128)(2,1)S(1)} collective-permute-done((bf16[16,32,128]{2,1,0:T(8,128)(2,1)S(1)}, bf16[16,32,128]{2,1,0:T(8,128)(2,1)S(1)}, u32[]{:S(2)}, u32[]{:S(2)}) %collective-permute-start) | collective-permute-done | bytes 131104 | tf_op jit(solution)/shard_map/ppermute | solution.py:13
  36.5 1.3 %collective-permute-start.1 = (bf16[16,32,128]{2,1,0:T(8,128)(2,1)S(1)}, bf16[16,32,128]{2,1,0:T(8,128)(2,1)S(1)}, u32[]{:S(2)}, u32[]{:S(2)}) collective-permute-start(bf16[16,32,128]{2,1,0:T(8,128)(2,1)S(1)} %collective-permute-done), channel_id=1, source_target_pairs={{0,24},{4,28},{8,0},{12,4},{16,8},{20,12},{24,16},{28,20},{1,25},{... | collective-permute-start | bytes 393224 | tf_op jit(solution)/shard_map/ppermute | solution.py:13
  37.9 4.7 %collective-permute-done.1 = bf16[16,32,128]{2,1,0:T(8,128)(2,1)S(1)} collective-permute-done((bf16[16,32,128]{2,1,0:T(8,128)(2,1)S(1)}, bf16[16,32,128]{2,1,0:T(8,128)(2,1)S(1)}, u32[]{:S(2)}, u32[]{:S(2)}) %collective-permute-start.1) | collective-permute-done | bytes 131104 | tf_op jit(solution)/shard_map/ppermute | solution.py:13
  42.5 0.3 collective-permute-start.2
  42.9 0.1 sine_negate_fusion
  43.0 4.8 %collective-permute-done.2 = bf16[16,32,128]{2,1,0:T(8,128)(2,1)S(1)} collective-permute-done((bf16[16,32,128]{2,1,0:T(8,128)(2,1)S(1)}, bf16[16,32,128]{2,1,0:T(8,128)(2,1)S(1)}, u32[]{:S(2)}, u32[]{:S(2)}) %collective-permute-start.2) | collective-permute-done | bytes 131104 | tf_op jit(solution)/shard_map/ppermute | solution.py:13
  47.8 0.2 multiply_reduce_fusion.2
  48.0 0.2 collective-permute-start.3
  48.3 0.4 copy.23
  48.9 0.4 copy.20
  49.3 0.4 convolution_bitcast_fusion.2
  49.8 0.3 copy.22
  50.1 0.4 convolution_bitcast_fusion.3
  50.6 0.3 copy.21
  50.9 0.3 fusion.5
  51.2 0.3 fusion.39
  51.7 0.4 copy.26
  52.1 1.4 %fusion.40 = f32[128,32,16]{1,2,0:T(8,128)} fusion(bf16[16,16,128]{1,0,2:T(8,128)(2,1)S(1)} %copy.26, bf16[16,32,128]{1,0,2:T(8,128)(2,1)S(1)} %copy.20), kind=kOutput, calls=%fused_computation.77 | convolution fusion | flops 2097152 | bytes 458752 | tf_op jit(solution)/shard_map/ijc,jrc->irc/dot_general | solution.py:67
  53.6 1.2 %copy.24 = bf16[16,16,128]{1,0,2:T(8,128)(2,1)} copy(bf16[16,16,128]{2,1,0:T(8,128)(2,1)S(1)} %pad_maximum_fusion.2) | data formatting | bytes 131072 | tf_op jit(solution)/shard_map/concatenate | solution.py:62
  55.1 0.4 copy.28
  55.5 0.4 convolution_bitcast_fusion
  56.0 0.3 copy.30
  56.3 0.4 copy.31
  56.7 0.4 convolution_bitcast_fusion.1
  57.2 0.3 copy.29
  57.5 0.2 multiply_reduce_fusion.1
  57.7 0.3 fusion.9
  58.0 0.3 fusion.38
  58.5 0.4 copy.34
  58.9 0.4 fusion.41
  59.4 0.4 copy.32
  59.9 0.4 convolution_add_fusion
  60.3 0.8 copy-done
  61.1 0.1 copy-done.1
  61.2 0.4 fusion.1
  61.6 1.1 %copy.35 = f32[16,32,128]{2,1,0:T(8,128)} copy(f32[16,32,128]{1,0,2:T(8,128)S(1)} %fusion.1) | data formatting | bytes 524288 | tf_op jit(solution)/shard_map/add | solution.py:120
  62.8 0.6 dynamic-slice
  64.0 0.2 slice_reduce_fusion.1
  64.2 0.2 slice_reduce_fusion
  64.4 10.6 %all-reduce = f32[16]{0:T(128)S(1)} all-reduce(f32[16]{0:T(128)S(1)} %add.84), channel_id=3, replica_groups=mesh['blk'=8,'off'=4] {'off'}, use_global_device_ids=true, to_apply=%region_6.7.clone | all-reduce | flops 16 | bytes 128
  75.0 0.6 fusion.33
  75.6 7.2 %reduce-scatter.2.cloned.1.call-done = f32[4,32,128]{2,1,0:T(8,128)} async-done(((f32[16,32,128]{2,1,0:T(8,128)}), f32[4,32,128]{2,1,0:T(8,128)}) %reduce-scatter.2.cloned.1.call-update) | async-done | bytes 65552 | tf_op jit(solution)/shard_map/reduce_scatter | solution.py:123
  82.8 1.5 %broadcast_divide_fusion = f32[4,32,128]{2,1,0:T(8,128)} fusion(f32[4,32,128]{2,1,0:T(8,128)} %reduce-scatter.2.cloned.1.call-done, f32[4]{0:T(128)S(1)} %get-tuple-element.5), kind=kLoop, calls=%fused_computation.48 | loop fusion | flops 16384 | bytes 131088 | tf_op jit(solution)/shard_map/div | solution.py:126
  (28 shorter events, 1.4 us)
Async XLA Ops:
  7.2 75.7 %reduce-scatter.2.cloned.1.call-start = ((), (), s32[]{:S(2)}) async-start(), calls=%async_computation.1 | async-start | bytes 327680 | tf_op jit(solution)/shard_map/reduce_scatter | solution.py:123
  32.8 3.7 %collective-permute-start = (bf16[16,32,128]{2,1,0:T(8,128)(2,1)S(1)}, bf16[16,32,128]{2,1,0:T(8,128)(2,1)S(1)}, u32[]{:S(2)}, u32[]{:S(2)}) collective-permute-start(bf16[16,32,128]{2,1,0:T(8,128)(2,1)S(1)} %copy.18), channel_id=1, source_target_pairs={{0,28},{4,0},{8,4},{12,8},{16,12},{20,16},{24,20},{28,24},{1,29},{... | collective-permute-start | bytes 393224 | tf_op jit(solution)/shard_map/ppermute | solution.py:13
  36.5 6.0 %collective-permute-start.1 = (bf16[16,32,128]{2,1,0:T(8,128)(2,1)S(1)}, bf16[16,32,128]{2,1,0:T(8,128)(2,1)S(1)}, u32[]{:S(2)}, u32[]{:S(2)}) collective-permute-start(bf16[16,32,128]{2,1,0:T(8,128)(2,1)S(1)} %collective-permute-done), channel_id=1, source_target_pairs={{0,24},{4,28},{8,0},{12,4},{16,8},{20,12},{24,16},{28,20},{1,25},{... | collective-permute-start | bytes 393224 | tf_op jit(solution)/shard_map/ppermute | solution.py:13
  42.5 5.2 %collective-permute-start.2 = (bf16[16,32,128]{2,1,0:T(8,128)(2,1)S(1)}, bf16[16,32,128]{2,1,0:T(8,128)(2,1)S(1)}, u32[]{:S(2)}, u32[]{:S(2)}) collective-permute-start(bf16[16,32,128]{2,1,0:T(8,128)(2,1)S(1)} %broadcast_select_fusion), channel_id=1, source_target_pairs={{0,16},{4,20},{8,24},{12,28},{16,0},{20,4},{24,8},{28,12},{1,17},{... | collective-permute-start | bytes 393224 | tf_op jit(solution)/shard_map/ppermute | solution.py:13
  48.0 6.8 %collective-permute-start.3 = (bf16[16,32,128]{2,1,0:T(8,128)(2,1)S(1)}, bf16[16,32,128]{2,1,0:T(8,128)(2,1)S(1)}, u32[]{:S(2)}, u32[]{:S(2)}) collective-permute-start(bf16[16,32,128]{2,1,0:T(8,128)(2,1)S(1)} %get-tuple-element.7), channel_id=1, source_target_pairs={{0,4},{4,8},{8,12},{12,16},{16,20},{20,24},{24,28},{28,0},{1,5},{5... | collective-permute-start | bytes 393224 | tf_op jit(solution)/shard_map/ppermute | solution.py:13
  59.9 1.2 %copy-start = (f32[128,32,16]{1,2,0:T(8,128)S(1)}, f32[128,32,16]{1,2,0:T(8,128)}, u32[]{:S(2)}) copy-start(f32[128,32,16]{1,2,0:T(8,128)} %fusion.40) | copy-start | bytes 786436
  59.9 1.3 %copy-start.1 = (bf16[16,16,128]{1,0,2:T(8,128)(2,1)S(1)}, bf16[16,16,128]{1,0,2:T(8,128)(2,1)}, u32[]{:S(2)}) copy-start(bf16[16,16,128]{1,0,2:T(8,128)(2,1)} %copy.24) | copy-start | bytes 196612
  61.6 1.2 %copy-start.2 = (u32[32]{0:T(128)S(1)}, u32[32]{0:T(128)}, u32[]{:S(2)}) copy-start(u32[32]{0:T(128)} %constant.70) | copy-start | bytes 388
Sparse Core Ops, SparseCore 0:
  62.9 19.8 reduce-scatter.1
where the time goes:
time: 91.5 us; the launch traced here: 91.2 us
  blocking collectives  34 us (37%)
  waiting for transfers between devices  18.7 us (20%)
  between operations  15 us (16%)
  local copies, waits for them, and re-layouts  10.9 us (12%)
  matrix products  5.46 us (6%)
  other arithmetic  4.18 us (5%)
  starting transfers between devices  3.05 us (3%)
    all_gather x1, blocking collectives, body(): own_block = lax.all_gather(coefficients, 'off', axis=1, tiled=True)  23.4 us
    ppermute x4, waiting for transfers between devices, shifted(): lax.ppermute(array, axis, [(i, (i + by) % count) for i in range(count)])  11.4 us
    unnamed x1, blocking collectives  10.6 us
    reduce_scatter x1, waiting for transfers between devices, body(): lax.psum_scatter(filtered, 'off', scatter_dimension=0, tiled=True)  7.22 us
    ppermute x4, starting transfers between devices, shifted(): lax.ppermute(array, axis, [(i, (i + by) % count) for i in range(count)])  3.02 us
    unnamed x8, local copies, waits for them, and re-layouts  2.54 us
  transfers between devices with their start and end apart: 5, of which 4 were waited for; matrix products, arithmetic and copies ran while one was open for 10% of the time, Pallas kernels for 0%

commit v1 on v0

--- a/solution.py
+++ b/solution.py
@@ -71,7 +71,16 @@
 
 
 def body(coefficients):
-    own_block = lax.all_gather(coefficients, "off", axis=1, tiled=True)
+    ways = lax.axis_size("off")
+    up = [(d, (d + 1) % ways) for d in range(ways)]
+    down = [(d, (d - 1) % ways) for d in range(ways)]
+    earlier, later = ([coefficients], [coefficients])
+    for _ in range(ways // 2):
+        earlier.append(lax.ppermute(earlier[-1], "off", up))
+    for _ in range((ways - 1) // 2):
+        later.append(lax.ppermute(later[-1], "off", down))
+    line = jnp.concatenate([*earlier[::-1], *later[1:]], axis=1)
+    own_block = jnp.roll(line, (lax.axis_index("off") - ways // 2) * coefficients.shape[1], axis=1)
     own_inverse = inverse_norms(own_block)
     row_count, radial, angular = own_block.shape
     forward, backward = angle_tables(angular)

time: 91.5 us -> 134 us (1.46)
  waiting for transfers between devices: 18.7 us -> 73.2 us
  blocking collectives: 34 us -> 10.1 us
  starting transfers between devices: 3.05 us -> 8.82 us
  local copies, waits for them, and re-layouts: 10.9 us -> 16 us
  other arithmetic: 4.18 us -> 5.66 us
    ppermute x0 -> x3, waiting for transfers between devices: none -> 34.4 us  [the longest x2 24.4 us: body(): earlier.append(lax.ppermute(earlier[-1], 'off', up))]
    all_gather x1 -> x0, blocking collectives: 23.4 us -> none  [body(): own_block = lax.all_gather(coefficients, 'off', axis=1, tiled=True)]
    ppermute x4, waiting for transfers between devices: 11.4 us -> 31.9 us  [shifted(): lax.ppermute(array, axis, [(i, (i + by) % count) for i in range(count)])]
    ppermute x0 -> x3, starting transfers between devices: none -> 5.17 us  [the longest x2 3.08 us: body(): earlier.append(lax.ppermute(earlier[-1], 'off', up))]
    concatenate x2 -> x1, local copies, waits for them, and re-layouts: 0.86 us -> 5.3 us  [body(): jnp.roll(line, (lax.axis_index('off') - ways // 2) * coefficients.shape[1...]
  transfers between devices with their start and end apart: 5 -> 8, of which waited for: 4 -> 8; matrix products, arithmetic and copies ran while one was open for 10% -> 8% of each run, Pallas kernels for 0% -> 0%
where the time goes in v1:
time: 134 us
  waiting for transfers between devices  73.2 us (55%)
  local copies, waits for them, and re-layouts  16 us (12%)
  between operations  14.9 us (11%)
  blocking collectives  10.1 us (8%)
  starting transfers between devices  8.82 us (7%)
  other arithmetic  5.66 us (4%)
  matrix products  5.34 us (4%)
    ppermute x4, waiting for transfers between devices, shifted(): lax.ppermute(array, axis, [(i, (i + by) % count) for i in range(count)])  31.9 us
    ppermute x2, waiting for transfers between devices, body(): earlier.append(lax.ppermute(earlier[-1], 'off', up))  24.4 us
    unnamed x1, blocking collectives  10.1 us
    ppermute x1, waiting for transfers between devices, body(): later.append(lax.ppermute(later[-1], 'off', down))  10 us
    reduce_scatter x1, waiting for transfers between devices, body(): lax.psum_scatter(filtered, 'off', scatter_dimension=0, tiled=True)  6.85 us
    concatenate x1, local copies, waits for them, and re-layouts, body(): jnp.roll(line, (lax.axis_index('off') - ways // 2) * coefficients.shape[1...  5.3 us
    ppermute x4, starting transfers between devices, shifted(): lax.ppermute(array, axis, [(i, (i + by) % count) for i in range(count)])  3.62 us
    unnamed x8, local copies, waits for them, and re-layouts  3.35 us
  transfers between devices with their start and end apart: 8, of which 8 were waited for; matrix products, arithmetic and copies ran while one was open for 8% of the time, Pallas kernels for 0%

profile of v1, /device:TPU:0, one launch (start us, length us, event | category | flops | bytes accessed | tf_op | source)
XLA Modules:
  0.0 134.0 jit_solution(9230879188101240140)
XLA Ops:
  7.2 1.2 copy.33
  8.4 3.1 %collective-permute-start = (bf16[16,8,128]{1,0,2:T(8,128)(2,1)S(1)}, bf16[16,8,128]{1,0,2:T(8,128)(2,1)S(1)}, u32[]{:S(2)}, u32[]{:S(2)}) collective-permute-start(bf16[16,8,128]{1,0,2:T(8,128)(2,1)S(1)} %copy.33), channel_id=1, source_target_pairs={{0,1},{1,2},{2,3},{3,0},{4,5},{5,6},{6,7},{7,4},{8,9},{9,10},{10,1... | collective-permute-start | bytes 98312 | tf_op jit(solution)/shard_map/ppermute | solution.py:79
  11.5 2.1 %collective-permute-start.2 = (bf16[16,8,128]{1,0,2:T(8,128)(2,1)S(1)}, bf16[16,8,128]{1,0,2:T(8,128)(2,1)S(1)}, u32[]{:S(2)}, u32[]{:S(2)}) collective-permute-start(bf16[16,8,128]{1,0,2:T(8,128)(2,1)S(1)} %copy.33), channel_id=1, source_target_pairs={{0,3},{1,0},{2,1},{3,2},{4,7},{5,4},{6,5},{7,6},{8,11},{9,8},{10,9... | collective-permute-start | bytes 98312 | tf_op jit(solution)/shard_map/ppermute | solution.py:81
  13.6 12.7 %collective-permute-done = bf16[16,8,128]{1,0,2:T(8,128)(2,1)S(1)} collective-permute-done((bf16[16,8,128]{1,0,2:T(8,128)(2,1)S(1)}, bf16[16,8,128]{1,0,2:T(8,128)(2,1)S(1)}, u32[]{:S(2)}, u32[]{:S(2)}) %collective-permute-start) | collective-permute-done | bytes 32800 | tf_op jit(solution)/shard_map/ppermute | solution.py:79
  26.3 10.0 %collective-permute-done.2 = bf16[16,8,128]{1,0,2:T(8,128)(2,1)S(1)} collective-permute-done((bf16[16,8,128]{1,0,2:T(8,128)(2,1)S(1)}, bf16[16,8,128]{1,0,2:T(8,128)(2,1)S(1)}, u32[]{:S(2)}, u32[]{:S(2)}) %collective-permute-start.2) | collective-permute-done | bytes 32800 | tf_op jit(solution)/shard_map/ppermute | solution.py:81
  36.3 11.6 %collective-permute-done.1 = bf16[16,8,128]{1,0,2:T(8,128)(2,1)S(1)} collective-permute-done((bf16[16,8,128]{1,0,2:T(8,128)(2,1)S(1)}, bf16[16,8,128]{1,0,2:T(8,128)(2,1)S(1)}, u32[]{:S(2)}, u32[]{:S(2)}) %collective-permute-start.1) | collective-permute-done | bytes 32800 | tf_op jit(solution)/shard_map/ppermute | solution.py:79
  47.9 5.3 %concatenate.33 = bf16[16,64,128]{1,0,2:T(8,128)(2,1)S(1)} concatenate(bf16[16,8,128]{1,0,2:T(8,128)(2,1)S(1)} %collective-permute-done.1, bf16[16,8,128]{1,0,2:T(8,128)(2,1)S(1)} %collective-permute-done, bf16[16,8,128]{1,0,2:T(8,128)(2,1)S(1)} %copy.33, bf16[16,8,128]{1,0,2:T(8,128)(2,1)S(1)} %collective-permute-done.2, bf16[16,8,128]{1,0,2:T(8,128)(2,1)S(1)} %collective-permute-done.1, ...), dimensions={1} | concatenate | bytes 524288 | tf_op jit(solution)/shard_map/jit(_roll_dynamic)/concatenate | solution.py:83
  53.2 0.4 multiply_reduce_fusion.2
  53.7 6.7 %collective-permute-done.3 = bf16[16,32,128]{1,0,2:T(8,128)(2,1)S(1)} collective-permute-done((bf16[16,32,128]{1,0,2:T(8,128)(2,1)S(1)}, bf16[16,32,128]{1,0,2:T(8,128)(2,1)S(1)}, u32[]{:S(2)}, u32[]{:S(2)}) %collective-permute-start.3) | collective-permute-done | bytes 131104 | tf_op jit(solution)/shard_map/ppermute | solution.py:13
  60.4 2.4 %collective-permute-start.4 = (bf16[16,32,128]{1,0,2:T(8,128)(2,1)S(1)}, bf16[16,32,128]{1,0,2:T(8,128)(2,1)S(1)}, u32[]{:S(2)}, u32[]{:S(2)}) collective-permute-start(bf16[16,32,128]{1,0,2:T(8,128)(2,1)S(1)} %collective-permute-done.3), channel_id=1, source_target_pairs={{0,24},{4,28},{8,0},{12,4},{16,8},{20,12},{24,16},{28,20},{1,25},{... | collective-permute-start | bytes 393224 | tf_op jit(solution)/shard_map/ppermute | solution.py:13
  63.0 11.9 %collective-permute-done.4 = bf16[16,32,128]{1,0,2:T(8,128)(2,1)S(1)} collective-permute-done((bf16[16,32,128]{1,0,2:T(8,128)(2,1)S(1)}, bf16[16,32,128]{1,0,2:T(8,128)(2,1)S(1)}, u32[]{:S(2)}, u32[]{:S(2)}) %collective-permute-start.4) | collective-permute-done | bytes 131104 | tf_op jit(solution)/shard_map/ppermute | solution.py:13
  75.0 1.1 collective-permute-start.5
  76.1 12.9 %collective-permute-done.5 = bf16[16,32,128]{1,0,2:T(8,128)(2,1)S(1)} collective-permute-done((bf16[16,32,128]{1,0,2:T(8,128)(2,1)S(1)}, bf16[16,32,128]{1,0,2:T(8,128)(2,1)S(1)}, u32[]{:S(2)}, u32[]{:S(2)}) %collective-permute-start.5) | collective-permute-done | bytes 131104 | tf_op jit(solution)/shard_map/ppermute | solution.py:13
  89.0 0.4 multiply_reduce_fusion.1
  89.4 0.4 convolution_bitcast_fusion.3
  89.8 0.4 convolution_bitcast_fusion.2
  90.2 0.9 slice_subtract_fusion.1
  91.1 1.3 copy.38
  92.4 0.9 slice_add_fusion.1
  93.2 1.3 copy.37
  94.5 0.3 fusion.5
  94.9 0.3 fusion.45
  95.3 0.4 copy.40
  95.8 1.4 %fusion.11 = f32[128,32,16]{1,2,0:T(8,128)} fusion(bf16[16,16,128]{1,0,2:T(8,128)(2,1)S(1)} %copy.40, bf16[16,32,64]{1,0,2:T(8,128)(2,1)S(1)} %get-tuple-element.11, bf16[16,32,64]{1,0,2:T(8,128)(2,1)S(1)} %get-tuple-element.10), kind=kOutput, calls=%fused_computation.30 | convolution fusion | flops 2359296 | bytes 458752 | tf_op jit(solution)/shard_map/ijc,jrc->irc/dot_general | solution.py:67
  97.3 1.2 copy.39
  98.4 0.4 collective-permute-done.6
  98.9 0.4 convolution_bitcast_fusion
  99.4 0.3 copy.42
  99.6 0.4 convolution_bitcast_fusion.1
  100.1 0.3 copy.41
  100.4 0.3 multiply_reduce_fusion
  100.7 0.3 fusion.9
  101.0 0.3 fusion.44
  101.5 0.4 copy.44
  101.9 0.4 fusion.10
  102.4 0.4 copy.43
  102.9 0.4 convolution_add_fusion
  103.3 0.8 copy-done
  104.2 0.4 fusion.1
  104.6 1.1 copy.45
  105.8 0.6 copy-done.2
  106.4 0.6 dynamic-slice
  107.7 0.2 slice_reduce_fusion.1
  107.9 0.2 slice_reduce_fusion
  108.1 10.1 %all-reduce = f32[16]{0:T(128)S(1)} all-reduce(f32[16]{0:T(128)S(1)} %add.97), channel_id=3, replica_groups=mesh['blk'=8,'off'=4] {'off'}, use_global_device_ids=true, to_apply=%region_6.7.clone | all-reduce | flops 16 | bytes 128
  118.2 0.6 fusion.39
  118.8 6.9 %reduce-scatter.2.cloned.1.call-done = f32[4,32,128]{2,1,0:T(8,128)} async-done(((f32[16,32,128]{2,1,0:T(8,128)}), f32[4,32,128]{2,1,0:T(8,128)}) %reduce-scatter.2.cloned.1.call-update) | async-done | bytes 65552 | tf_op jit(solution)/shard_map/reduce_scatter | solution.py:132
  125.6 1.5 %broadcast_divide_fusion = f32[4,32,128]{2,1,0:T(8,128)} fusion(f32[4,32,128]{2,1,0:T(8,128)} %reduce-scatter.2.cloned.1.call-done, f32[4]{0:T(128)S(1)} %get-tuple-element.5), kind=kLoop, calls=%fused_computation.50 | loop fusion | flops 16384 | bytes 131088 | tf_op jit(solution)/shard_map/div | solution.py:135
  (27 shorter events, 1.3 us)
Async XLA Ops:
  7.2 118.5 %reduce-scatter.2.cloned.1.call-start = ((), (), s32[]{:S(2)}) async-start(), calls=%async_computation.1 | async-start | bytes 327680 | tf_op jit(solution)/shard_map/reduce_scatter | solution.py:132
  8.4 17.9 %collective-permute-start = (bf16[16,8,128]{1,0,2:T(8,128)(2,1)S(1)}, bf16[16,8,128]{1,0,2:T(8,128)(2,1)S(1)}, u32[]{:S(2)}, u32[]{:S(2)}) collective-permute-start(bf16[16,8,128]{1,0,2:T(8,128)(2,1)S(1)} %copy.33), channel_id=1, source_target_pairs={{0,1},{1,2},{2,3},{3,0},{4,5},{5,6},{6,7},{7,4},{8,9},{9,10},{10,1... | collective-permute-start | bytes 98312 | tf_op jit(solution)/shard_map/ppermute | solution.py:79
  11.5 24.8 %collective-permute-start.2 = (bf16[16,8,128]{1,0,2:T(8,128)(2,1)S(1)}, bf16[16,8,128]{1,0,2:T(8,128)(2,1)S(1)}, u32[]{:S(2)}, u32[]{:S(2)}) collective-permute-start(bf16[16,8,128]{1,0,2:T(8,128)(2,1)S(1)} %copy.33), channel_id=1, source_target_pairs={{0,3},{1,0},{2,1},{3,2},{4,7},{5,4},{6,5},{7,6},{8,11},{9,8},{10,9... | collective-permute-start | bytes 98312 | tf_op jit(solution)/shard_map/ppermute | solution.py:81
  26.3 21.6 %collective-permute-start.1 = (bf16[16,8,128]{1,0,2:T(8,128)(2,1)S(1)}, bf16[16,8,128]{1,0,2:T(8,128)(2,1)S(1)}, u32[]{:S(2)}, u32[]{:S(2)}) collective-permute-start(bf16[16,8,128]{1,0,2:T(8,128)(2,1)S(1)} %collective-permute-done), channel_id=1, source_target_pairs={{0,1},{1,2},{2,3},{3,0},{4,5},{5,6},{6,7},{7,4},{8,9},{9,10},{10,1... | collective-permute-start | bytes 98312 | tf_op jit(solution)/shard_map/ppermute | solution.py:79
  53.6 6.8 %collective-permute-start.3 = (bf16[16,32,128]{1,0,2:T(8,128)(2,1)S(1)}, bf16[16,32,128]{1,0,2:T(8,128)(2,1)S(1)}, u32[]{:S(2)}, u32[]{:S(2)}) collective-permute-start(bf16[16,32,128]{1,0,2:T(8,128)(2,1)S(1)} %get-tuple-element.9), channel_id=1, source_target_pairs={{0,28},{4,0},{8,4},{12,8},{16,12},{20,16},{24,20},{28,24},{1,29},{... | collective-permute-start | bytes 393224 | tf_op jit(solution)/shard_map/ppermute | solution.py:13
  60.4 14.5 %collective-permute-start.4 = (bf16[16,32,128]{1,0,2:T(8,128)(2,1)S(1)}, bf16[16,32,128]{1,0,2:T(8,128)(2,1)S(1)}, u32[]{:S(2)}, u32[]{:S(2)}) collective-permute-start(bf16[16,32,128]{1,0,2:T(8,128)(2,1)S(1)} %collective-permute-done.3), channel_id=1, source_target_pairs={{0,24},{4,28},{8,0},{12,4},{16,8},{20,12},{24,16},{28,20},{1,25},{... | collective-permute-start | bytes 393224 | tf_op jit(solution)/shard_map/ppermute | solution.py:13
  75.0 14.0 %collective-permute-start.5 = (bf16[16,32,128]{1,0,2:T(8,128)(2,1)S(1)}, bf16[16,32,128]{1,0,2:T(8,128)(2,1)S(1)}, u32[]{:S(2)}, u32[]{:S(2)}) collective-permute-start(bf16[16,32,128]{1,0,2:T(8,128)(2,1)S(1)} %broadcast_select_fusion), channel_id=1, source_target_pairs={{0,16},{4,20},{8,24},{12,28},{16,0},{20,4},{24,8},{28,12},{1,17},{... | collective-permute-start | bytes 393224 | tf_op jit(solution)/shard_map/ppermute | solution.py:13
  89.3 9.6 %collective-permute-start.6 = (bf16[16,32,128]{1,0,2:T(8,128)(2,1)S(1)}, bf16[16,32,128]{1,0,2:T(8,128)(2,1)S(1)}, u32[]{:S(2)}, u32[]{:S(2)}) collective-permute-start(bf16[16,32,128]{1,0,2:T(8,128)(2,1)S(1)} %get-tuple-element.7), channel_id=1, source_target_pairs={{0,4},{4,8},{8,12},{12,16},{16,20},{20,24},{24,28},{28,0},{1,5},{5... | collective-permute-start | bytes 393224 | tf_op jit(solution)/shard_map/ppermute | solution.py:13
  102.9 1.2 copy-start
  102.9 1.3 %copy-start.1 = (bf16[16,16,128]{1,0,2:T(8,128)(2,1)S(1)}, bf16[16,16,128]{1,0,2:T(8,128)(2,1)}, u32[]{:S(2)}) copy-start(bf16[16,16,128]{1,0,2:T(8,128)(2,1)} %copy.39) | copy-start | bytes 196612
  105.8 0.7 copy-start.2
Sparse Core Ops, SparseCore 0:
  105.9 19.6 reduce-scatter.1
